TPU v7x, 32 devices: a whole 2x2x4 slice. The times are simulated.
32 devices in a mesh: horiz: 8 (over z, y), vert: 4 (over x, core).
Axes of the slice: x: 2, y: 2, z: 4, core: 2. Of those that a mesh axis runs over, the one named last changes fastest.
Arguments:
- tracer: bfloat16 [8, 2048, 128], P('vert', 'horiz'), may hold values from -6 to 6
- explicit_tiles: bfloat16 [8, 16, 7, 128, 128], P('vert', 'horiz'), may hold values from -0.25 to 0.25
- tile_columns: int32 [8, 16, 7], P('vert', 'horiz'), may hold values from 0 to 127, as said below
- tile_counts: int32 [8, 16], P('vert', 'horiz'), may hold values from 4 to 7
- surface_source: bfloat16 [2048, 128], P('horiz'), may hold values from -6 to 6
- implicit_columns: float32 [2048, 8, 8], P(('horiz', 'vert')), may hold values from -0.53033009 to 1
- settling: float32 [128], replicated, may hold values from 0.02 to 0.5
- wet_mask: int32 [8, 2048], P('vert', 'horiz'), may hold values 0 or 1
Outputs:
- tracer_out: bfloat16 [8, 2048, 128], P('vert', 'horiz')
Inputs may be any that keep to these rules, and one draw needn't show every extreme that they name: `tile_columns`: slot 0 of block row (l, t) names the row's own tile l * 16 + t; the other slots name distinct tiles within 2 levels and 2 tiles of it, inside the grid.
All inputs are finite; a program needn't handle non-finite values. No bound on the sum of `wet_mask` on one device may be relied on, other than what follows from the above.
Results may differ from a plain program's by a relative error of at most 0.015.
Values may be sent and summed in bfloat16 or wider, within the bound.
A program may use at most 64 MiB of HBM per device.

v0:
```python
import functools

import jax
import jax.numpy as jnp
from jax import lax
from jax.experimental import pallas as pl
from jax.experimental.pallas import tpu as pltpu
from jax.sharding import PartitionSpec as P

REACH = 2
STEPS = 4
Q = 4
MESH = pl.DeviceIdType.MESH
F32 = jnp.float32
BF16 = jnp.bfloat16


def kernel(
    h_size,
    v_size,
    tracer,
    tiles,
    source,
    extra,
    settling,
    columns,
    counts,
    out,
    weights,
    turned,
    gath,
    other,
    final,
    src_t,
    fall,
    ops,
    a_win,
    w_win,
    cols_v,
    cols_s,
    pos,
    send_sem,
    recv_sem,
    first_send,
    first_recv,
    last_send,
    last_recv,
    ops_send,
    ops_recv,
    pair_send,
    pair_recv,
    local_sem,
    *halos,
):
    lev_dev, cells_dev, classes = tracer.shape
    slots, size = tiles.shape[2], tiles.shape[3]
    tiles_dev = cells_dev // size
    window = lev_dev + 2 * REACH
    levels = lev_dev * v_size
    lev_chip = 2 * lev_dev
    h_tiles = h_size * tiles_dev
    half = classes // 2
    ch = half // Q
    blk = tiles_dev * window
    h = lax.axis_index("horiz")
    v = lax.axis_index("vert")
    even = lax.rem(h, 2) == 0
    core = lax.rem(v, 2)
    chip = v // 2
    base = 2 * chip
    partner = jnp.where(even, h + 1, h - 1)
    ahead = jnp.where(even, h + 2, h - 2)
    behind = jnp.where(even, h - 2, h + 2)
    has_ahead = (ahead >= 0) & (ahead < h_size)
    has_behind = (behind >= 0) & (behind < h_size)

    def vert(d):
        flipped = v
        if d & 1:
            flipped = flipped + 1 - 2 * core
        if d & 2:
            flipped = lax.rem(flipped + 2, 4)
        return {"horiz": h, "vert": flipped}

    near = {"horiz": partner, "vert": v}
    front = {"horiz": ahead, "vert": v}
    back = {"horiz": behind, "vert": v}

    barrier = pltpu.get_barrier_semaphore()
    for where in (vert(1), vert(2), vert(3), near):
        pl.semaphore_signal(barrier, inc=1, device_id=where, device_id_type=MESH)

    @pl.when(has_ahead)
    def _():
        pl.semaphore_signal(barrier, inc=1, device_id=front, device_id_type=MESH)

    @pl.when(has_behind)
    def _():
        pl.semaphore_signal(barrier, inc=1, device_id=back, device_id_type=MESH)

    near_at = jnp.where(even, 2 * blk, 0)
    far_at = jnp.where(even, 0, 2 * blk)

    def copy_to(src, dst, send, recv, where):
        return pltpu.make_async_remote_copy(
            src_ref=src,
            dst_ref=dst,
            send_sem=send,
            recv_sem=recv,
            device_id=where,
            device_id_type=MESH,
        )

    def remote(src, dst, p, q, kind, where):
        return copy_to(
            src, dst, send_sem.at[p, q, kind], recv_sem.at[p, q, kind], where
        )

    def x_copies(p, q):
        if p == 0:
            here = gath.at[0, q, pl.ds(lev_dev * v, lev_dev)]
            return [
                copy_to(
                    here if d == 2 else other.at[q],
                    here,
                    first_send.at[q, d - 1],
                    first_recv.at[q, d - 1],
                    vert(d),
                )
                for d in (2, 3, 1)
            ]
        here = gath.at[p % 2, q, pl.ds(lev_chip * chip, lev_chip)]
        return [remote(here, here, p, q, 0, vert(2))]

    def block(p, q, at):
        return halos[p % 2 * Q + q].at[pl.ds(at, blk)]

    def near_copy(p, q):
        return remote(block(p, q, blk), block(p, q, far_at), p, q, 1, near)

    def front_copy(p, q):
        return remote(block(p, q, near_at), block(p, q, far_at), p, q, 2, front)

    def last_copies(q):
        theirs = lev_dev * (v + 1 - 2 * core) - base
        halo = halos[STEPS % 2 * Q + q]
        return [
            copy_to(
                halo.at[pl.ds(blk + t * window + theirs, lev_dev)],
                final.at[core * Q + q, t],
                last_send.at[q, t],
                last_recv.at[q, t],
                vert(1),
            )
            for t in range(tiles_dev)
        ]

    def pair_copies():
        mine = weights.at[pl.ds(lev_dev * core, lev_dev)]
        cols = cols_v.at[core]
        return [
            copy_to(cols, cols, pair_send.at[0], pair_recv.at[0], vert(1)),
            copy_to(mine, mine, pair_send.at[1], pair_recv.at[1], vert(1)),
        ]

    def load_first(q):
        for level in range(lev_dev):
            for t in range(tiles_dev):
                ours = pl.ds(pl.multiple_of(core * half + q * ch, ch), ch)
                theirs = pl.ds(pl.multiple_of((1 - core) * half + q * ch, ch), ch)
                gath[0, q, lev_dev * v + level, t] = turned[level, t, ours, :]
                other[q, level, t] = turned[level, t, theirs, :]

    def explicit(p, q):
        for level in range(lev_chip):
            for t in range(tiles_dev):
                picked = jnp.concatenate(
                    [
                        halos[(p - 1) % 2 * Q + q][pos[level, t * slots + j]]
                        for j in range(slots)
                    ],
                    axis=1,
                )
                flow = jnp.dot(
                    picked, weights[level, t], preferred_element_type=F32
                )
                if level == 0:
                    ours = pl.ds(pl.multiple_of(core * half + q * ch, ch), ch)
                    flow = flow + src_t[t, ours, :]
                gath[p % 2, q, lev_chip * chip + level, t] = flow.astype(BF16)

    def stage_a(p, q):
        if p == 0:
            load_first(q)
        else:
            explicit(p, q)
        for copy in x_copies(p, q):
            copy.start()

    def sends_done(p, q):
        for copy in x_copies(p, q):
            copy.wait_send()
        if p == STEPS:
            return
        near_copy(p, q).wait_send()

        @pl.when(has_ahead)
        def _():
            front_copy(p, q).wait_send()

    def solve(p, q):
        par = p % 2
        halo = halos[par * Q + q]
        if p == 0:
            for t in range(tiles_dev):
                for k in range(window):
                    halo[blk + t * window + k] = gath[par, q, base + k, t]
            return
        rows = 16

        for t in range(tiles_dev):
            for i in range(ch // rows):
                at = slice(i * rows, (i + 1) * rows)
                loaded = [gath[par, q, m, t, at, :].astype(F32) for m in range(levels)]
                start = core * half + q * ch + i * rows
                rate = fall[pl.ds(pl.multiple_of(start, rows), rows), :]
                stay = 1.0 - rate
                above = None
                for k in range(window + 1):
                    mixed = None
                    for m in range(levels):
                        r = k * levels + m
                        term = a_win[t, r : r + 1, :] * loaded[m]
                        mixed = term if m == 0 else mixed + term
                    if k:
                        settled = stay * mixed + rate * above
                        wet = w_win[t, k - 1 : k, :]
                        halo[blk + t * window + k - 1, at, :] = (wet * settled).astype(BF16)
                    above = mixed

    def stage_b(p, q):
        for copy in x_copies(p, q):
            copy.wait_recv()
        if p:
            sends_done(p - 1, q)
        solve(p, q)
        if p < STEPS:
            near_copy(p, q).start()
        else:
            for copy in last_copies(q):
                copy.start()

    def stage_c(p, q):
        near_copy(p, q).wait_recv()

        @pl.when(has_ahead)
        def _():
            front_copy(p, q).start()

    def stage_d(p, q):
        @pl.when(has_behind)
        def _():
            front_copy(p, q).wait_recv()

    def ops_copy(d):
        return copy_to(
            extra, ops.at[v], ops_send.at[d - 1], ops_recv.at[d - 1], vert(d)
        )

    def prepare():
        for level in range(lev_dev):
            for t in range(tiles_dev):
                for j in range(slots):
                    live = (j < counts[level, t]).astype(F32)
                    weights[lev_dev * core + level, t, j * size : (j + 1) * size, :] = (
                        tiles[level, t, j].astype(F32).T * live
                    ).astype(BF16)

    def prepare_more():
        on_top = (chip == 0).astype(F32)
        for t in range(tiles_dev):
            src_t[t] = source[t * size : (t + 1) * size, :].astype(F32).T * on_top
        fall[...] = jnp.broadcast_to(settling[...], (size, classes)).T

    def positions():
        local = pltpu.make_async_copy(cols_v, cols_s, local_sem)
        local.start()
        local.wait()
        last = 3 * blk - 1
        for level in range(lev_chip):
            for n in range(tiles_dev * slots):
                column = cols_s[level // lev_dev, level % lev_dev, n]
                row = lax.div(column, h_tiles) - base
                across = lax.rem(column, h_tiles) - tiles_dev * h + REACH
                pos[level, n] = jnp.clip(across * window + row, 0, last)

    def operators():
        square = levels * levels
        for t in range(tiles_dev):
            for k in range(window + 1):
                level = base + k - 1
                row = pl.ds(
                    pl.multiple_of(jnp.maximum(level, 0) * levels, levels), levels
                )
                keep = (level >= 0).astype(F32)
                a_win[t, k * levels : (k + 1) * levels, :] = keep * (
                    ops[2 * t, row, :] + ops[2 * t + 1, row, :]
                )
                if k:
                    w_win[t, k - 1 : k, :] = ops[
                        level // lev_dev,
                        pl.ds(square + lax.rem(level, lev_dev) * tiles_dev + t, 1),
                        :,
                    ]

    ops[v] = extra[...]
    cols_v[core] = columns[...]
    for level in range(lev_dev):
        for t in range(tiles_dev):
            turned[level, t] = tracer[level, t * size : (t + 1) * size, :].T
    count = 4 + has_ahead.astype(jnp.int32) + has_behind.astype(jnp.int32)
    pl.semaphore_wait(barrier, count)
    for q in range(Q):
        stage_a(0, q)
    for d in (1, 2, 3):
        ops_copy(d).start()
    pair = pair_copies()
    pair[0].start()
    prepare()
    pair[1].start()
    for q in range(Q):
        stage_b(0, q)
    prepare_more()
    for d in (1, 2, 3):
        ops_copy(d).wait()
    operators()
    pair[0].wait()
    positions()
    for p in range(STEPS):
        for q in range(Q):
            stage_c(p, q)
        if p == 0:
            pair[1].wait()
        for q in range(Q):
            stage_d(p, q)
            stage_a(p + 1, q)
        for q in range(Q):
            stage_b(p + 1, q)
    mine = lev_dev * v - base
    for q in range(Q):
        for t in range(tiles_dev):
            for level in range(lev_dev):
                final[core * Q + q, t, level] = halos[STEPS % 2 * Q + q][
                    blk + t * window + mine + level
                ]
    for q in range(Q):
        for copy in last_copies(q):
            copy.wait_recv()
    for level in range(lev_dev):
        for t in range(tiles_dev):
            whole = jnp.concatenate(
                [final[i, t, level] for i in range(2 * Q)], axis=0
            )
            out[level, t * size : (t + 1) * size, :] = whole.T
    for q in range(Q):
        sends_done(STEPS, q)
        for copy in last_copies(q):
            copy.wait_send()


def on_device(h_size, v_size, tracer, tiles, columns, counts, source, implicit, settling, wet):
    lev_dev, cells_dev, classes = tracer.shape
    slots, size = tiles.shape[2], tiles.shape[3]
    tiles_dev = cells_dev // size
    levels = implicit.shape[1]
    share = implicit.shape[0]
    window = lev_dev + 2 * REACH
    assert lev_dev == 2 and tiles_dev == 2 and v_size == 4 and h_size % 2 == 0
    ch = classes // 2 // Q
    flat = implicit.reshape(share, levels * levels).T
    right = lax.rem(lax.axis_index("vert"), 2).astype(F32)
    flat = jnp.concatenate([flat * (1.0 - right), flat * right], axis=1)
    wet_rows = wet.astype(F32).reshape(lev_dev * tiles_dev, size)
    extra = jnp.concatenate([flat, wet_rows, jnp.zeros_like(wet_rows)], axis=0)
    vm = pl.BlockSpec(memory_space=pltpu.VMEM)
    sm = pl.BlockSpec(memory_space=pltpu.SMEM)
    phases = STEPS + 1
    cols = columns.reshape(lev_dev, tiles_dev * slots)
    cols = jnp.pad(cols, ((0, 8 - lev_dev), (0, 128 - cols.shape[1])))
    dma = pltpu.SemaphoreType.DMA
    return pl.pallas_call(
        functools.partial(kernel, h_size, v_size),
        out_shape=jax.ShapeDtypeStruct(tracer.shape, tracer.dtype),
        in_specs=[vm] * 6 + [sm],
        out_specs=vm,
        scratch_shapes=[
            pltpu.VMEM((2 * lev_dev, tiles_dev, slots * size, size), BF16),
            pltpu.VMEM((lev_dev, tiles_dev, classes, size), BF16),
            pltpu.VMEM((2, Q, levels, tiles_dev, ch, size), BF16),
            pltpu.VMEM((Q, lev_dev, tiles_dev, ch, size), BF16),
            pltpu.VMEM((2 * Q, tiles_dev, lev_dev, ch, size), BF16),
            pltpu.VMEM((tiles_dev, classes, size), F32),
            pltpu.VMEM((classes, size), F32),
            pltpu.VMEM((v_size,) + extra.shape, F32),
            pltpu.VMEM((tiles_dev, (window + 1) * levels, size), F32),
            pltpu.VMEM((tiles_dev, 8, size), F32),
            pltpu.VMEM((2,) + cols.shape, jnp.int32),
            pltpu.SMEM((2,) + cols.shape, jnp.int32),
            pltpu.SMEM((2 * lev_dev, tiles_dev * slots), jnp.int32),
            dma((phases, Q, 3)),
            dma((phases, Q, 3)),
            dma((Q, 3)),
            dma((Q, 3)),
            dma((Q, tiles_dev)),
            dma((Q, tiles_dev)),
            dma((3,)),
            dma((3,)),
            dma((2,)),
            dma((2,)),
            dma(()),
        ]
        + [pltpu.VMEM((3 * tiles_dev * window, ch, size), BF16)] * (2 * Q),
        compiler_params=pltpu.CompilerParams(
            collective_id=0, has_side_effects=True, vmem_limit_bytes=32 * 2**20
        ),
    )(tracer, tiles, source, extra, settling.reshape(1, classes), cols, counts)


def solution(mesh):
    placed = (
        P("vert", "horiz", None),
        P("vert", "horiz", None, None, None),
        P("vert", "horiz", None),
        P("vert", "horiz"),
        P("horiz", None),
        P(("horiz", "vert"), None, None),
        P(),
        P("vert", "horiz"),
    )
    body = functools.partial(on_device, mesh.shape["horiz"], mesh.shape["vert"])
    return jax.shard_map(
        body, mesh=mesh, in_specs=placed, out_specs=P("vert", "horiz", None), check_vma=False
    )
```

profile of v0, /device:TPU:0, one launch (start us, length us, event | category | flops | bytes accessed | tf_op | source)
XLA Modules:
  0.0 55.1 jit_solution(16427221412896914388)
XLA Ops:
  0.0 0.0 copy-start.5
  0.0 0.0 copy-start.1
  0.0 0.1 pad.8.clone
  0.1 0.8 %reshape.16 = s32[2,14]{1,0:T(2,128)S(1)} reshape(s32[2,2,7]{2,1,0:T(2,128)} %param.10) | data formatting | bytes 224 | tf_op jit(solution)/shard_map/reshape | solution.py:388
  0.8 0.7 %convert_element_type.7 = f32[2,256]{1,0:T(2,128)S(1)} convert(s32[2,256]{1,0:T(2,128)} %param.15) | non-fusion elementwise | flops 512 | bytes 4096 | tf_op jit(solution)/shard_map/convert_element_type | solution.py:383
  1.6 0.0 copy-done.5
  1.6 0.0 copy-start.2
  1.6 0.0 copy-start.3
  1.6 0.0 copy-start.4
  1.6 0.1 maximum_maximum_fusion.extra
  1.7 0.0 copy-done.1
  1.7 0.7 %copy-done.2 = bf16[256,128]{1,0:T(8,128)(2,1)S(1)} copy-done((bf16[256,128]{1,0:T(8,128)(2,1)S(1)}, bf16[256,128]{1,0:T(8,128)(2,1)}, u32[]{:S(2)}) %copy-start.2) | copy-done | bytes 65560
  2.4 0.0 copy-done.3
  2.4 0.0 copy-done.4
  2.4 0.0 copy-start
  2.4 1.2 %copy-done = bf16[2,2,7,128,128]{4,3,2,1,0:T(8,128)(2,1)S(1)} copy-done((bf16[2,2,7,128,128]{4,3,2,1,0:T(8,128)(2,1)S(1)}, bf16[2,2,7,128,128]{4,3,2,1,0:T(8,128)(2,1)}, u32[]{:S(2)}) %copy-start) | copy-done | bytes 917528
  3.6 50.9 %shard_map.82 = bf16[2,256,128]{2,1,0:T(8,128)(2,1)S(1)} custom-call(bf16[2,256,128]{2,1,0:T(8,128)(2,1)S(1)} %copy-done.1, bf16[2,2,7,128,128]{4,3,2,1,0:T(8,128)(2,1)S(1)} %copy-done, bf16[256,128]{1,0:T(8,128)(2,1)S(1)} %copy-done.2, f32[72,128]{1,0:T(8,128)S(1)} %maximum_maximum_fusion.extra, f32[1,128]{1,0:T(1,128)S(1)} %bitcast.9, ...), custom_call_target="tpu_custom_call" | custom-call | tf_op jit(solution)/shard_map/pallas_call | solution.py:391
  54.5 0.7 %copy.10 = bf16[2,256,128]{2,1,0:T(8,128)(2,1)} copy(bf16[2,256,128]{2,1,0:T(8,128)(2,1)S(1)} %shard_map.82) | data formatting | bytes 262144
  (4 shorter events, 0.0 us)
Async XLA Ops:
  0.0 1.6 %copy-start.5 = (f32[64,8,8]{0,2,1:T(8,128)S(1)}, f32[64,8,8]{0,2,1:T(8,128)}, u32[]{:S(2)}) copy-start(f32[64,8,8]{0,2,1:T(8,128)} %param.13) | copy-start | bytes 49156
  0.0 1.7 %copy-start.1 = (bf16[2,256,128]{2,1,0:T(8,128)(2,1)S(1)}, bf16[2,256,128]{2,1,0:T(8,128)(2,1)}, u32[]{:S(2)}) copy-start(bf16[2,256,128]{2,1,0:T(8,128)(2,1)} %tracer.1) | copy-start | bytes 393220
  1.6 0.8 %copy-start.2 = (bf16[256,128]{1,0:T(8,128)(2,1)S(1)}, bf16[256,128]{1,0:T(8,128)(2,1)}, u32[]{:S(2)}) copy-start(bf16[256,128]{1,0:T(8,128)(2,1)} %source.1) | copy-start | bytes 196612
  1.6 0.8 %copy-start.3 = (s32[2,2]{1,0:T(2,128)S(1)}, s32[2,2]{1,0:T(2,128)}, u32[]{:S(2)}) copy-start(s32[2,2]{1,0:T(2,128)} %counts.1) | copy-start | bytes 52
  1.6 0.8 %copy-start.4 = (f32[128]{0:T(128)S(1)}, f32[128]{0:T(128)}, u32[]{:S(2)}) copy-start(f32[128]{0:T(128)} %param.14) | copy-start | bytes 1540
  2.4 1.2 %copy-start = (bf16[2,2,7,128,128]{4,3,2,1,0:T(8,128)(2,1)S(1)}, bf16[2,2,7,128,128]{4,3,2,1,0:T(8,128)(2,1)}, u32[]{:S(2)}) copy-start(bf16[2,2,7,128,128]{4,3,2,1,0:T(8,128)(2,1)} %tiles.1) | copy-start | bytes 2752516
where the time goes:
time: 55.9 us; the launch traced here: 55.1 us
  Pallas kernels  50.9 us (91%)
  local copies, waits for them, and re-layouts  3.43 us (6%)
  other arithmetic  0.78 us (1%)
    pallas_call x1, Pallas kernels, on_device(): pl.pallas_call(functools.partial(kernel, h_size, v_size), out_shape=jax.S...  50.9 us
    unnamed x13, local copies, waits for them, and re-layouts  2.57 us

commit v1 on v0

--- a/solution.py
+++ b/solution.py
@@ -68,6 +68,7 @@
     core = lax.rem(v, 2)
     chip = v // 2
     base = 2 * chip
+    part = lax.rem(core + chip + h // 2 + lax.rem(h, 2), 2)
     partner = jnp.where(even, h + 1, h - 1)
     ahead = jnp.where(even, h + 2, h - 2)
     behind = jnp.where(even, h - 2, h + 2)
@@ -82,9 +83,10 @@
             flipped = lax.rem(flipped + 2, 4)
         return {"horiz": h, "vert": flipped}
 
-    near = {"horiz": partner, "vert": v}
-    front = {"horiz": ahead, "vert": v}
-    back = {"horiz": behind, "vert": v}
+    crossed = v + 1 - 2 * core
+    near = {"horiz": partner, "vert": crossed}
+    front = {"horiz": ahead, "vert": crossed}
+    back = {"horiz": behind, "vert": crossed}
 
     barrier = pltpu.get_barrier_semaphore()
     for where in (vert(1), vert(2), vert(3), near):
@@ -121,16 +123,16 @@
             here = gath.at[0, q, pl.ds(lev_dev * v, lev_dev)]
             return [
                 copy_to(
-                    here if d == 2 else other.at[q],
+                    here if d == 3 else other.at[q],
                     here,
                     first_send.at[q, d - 1],
                     first_recv.at[q, d - 1],
                     vert(d),
                 )
-                for d in (2, 3, 1)
+                for d in (3, 2, 1)
             ]
         here = gath.at[p % 2, q, pl.ds(lev_chip * chip, lev_chip)]
-        return [remote(here, here, p, q, 0, vert(2))]
+        return [remote(here, here, p, q, 0, vert(3))]
 
     def block(p, q, at):
         return halos[p % 2 * Q + q].at[pl.ds(at, blk)]
@@ -147,7 +149,7 @@
         return [
             copy_to(
                 halo.at[pl.ds(blk + t * window + theirs, lev_dev)],
-                final.at[core * Q + q, t],
+                final.at[part * Q + q, t],
                 last_send.at[q, t],
                 last_recv.at[q, t],
                 vert(1),
@@ -166,8 +168,8 @@
     def load_first(q):
         for level in range(lev_dev):
             for t in range(tiles_dev):
-                ours = pl.ds(pl.multiple_of(core * half + q * ch, ch), ch)
-                theirs = pl.ds(pl.multiple_of((1 - core) * half + q * ch, ch), ch)
+                ours = pl.ds(pl.multiple_of(part * half + q * ch, ch), ch)
+                theirs = pl.ds(pl.multiple_of((1 - part) * half + q * ch, ch), ch)
                 gath[0, q, lev_dev * v + level, t] = turned[level, t, ours, :]
                 other[q, level, t] = turned[level, t, theirs, :]
 
@@ -185,7 +187,7 @@
                     picked, weights[level, t], preferred_element_type=F32
                 )
                 if level == 0:
-                    ours = pl.ds(pl.multiple_of(core * half + q * ch, ch), ch)
+                    ours = pl.ds(pl.multiple_of(part * half + q * ch, ch), ch)
                     flow = flow + src_t[t, ours, :]
                 gath[p % 2, q, lev_chip * chip + level, t] = flow.astype(BF16)
 
@@ -222,7 +224,7 @@
             for i in range(ch // rows):
                 at = slice(i * rows, (i + 1) * rows)
                 loaded = [gath[par, q, m, t, at, :].astype(F32) for m in range(levels)]
-                start = core * half + q * ch + i * rows
+                start = part * half + q * ch + i * rows
                 rate = fall[pl.ds(pl.multiple_of(start, rows), rows), :]
                 stay = 1.0 - rate
                 above = None
@@ -350,7 +352,7 @@
     for q in range(Q):
         for t in range(tiles_dev):
             for level in range(lev_dev):
-                final[core * Q + q, t, level] = halos[STEPS % 2 * Q + q][
+                final[part * Q + q, t, level] = halos[STEPS % 2 * Q + q][
                     blk + t * window + mine + level
                 ]
     for q in range(Q):

time: 55.9 us -> 57.1 us (1.021)
  Pallas kernels: 50.9 us -> 52.6 us
    pallas_call x1, Pallas kernels: 50.9 us -> 52.6 us  [on_device(): pl.pallas_call(functools.partial(kernel, h_size, v_size), out_shape=jax.S...]
where the time goes in v1:
time: 57.1 us; the launch traced here: 56.9 us
  Pallas kernels  52.6 us (92%)
  local copies, waits for them, and re-layouts  3.43 us (6%)
  other arithmetic  0.78 us (1%)
    pallas_call x1, Pallas kernels, on_device(): pl.pallas_call(functools.partial(kernel, h_size, v_size), out_shape=jax.S...  52.6 us
    unnamed x13, local copies, waits for them, and re-layouts  2.57 us

profile of v1, /device:TPU:0, one launch (start us, length us, event | category | flops | bytes accessed | tf_op | source)
XLA Modules:
  0.0 56.9 jit_solution(3187109750888335993)
XLA Ops:
  0.0 0.0 copy-start.5
  0.0 0.0 copy-start.1
  0.0 0.1 pad.8.clone
  0.1 0.8 %reshape.16 = s32[2,14]{1,0:T(2,128)S(1)} reshape(s32[2,2,7]{2,1,0:T(2,128)} %param.10) | data formatting | bytes 224 | tf_op jit(solution)/shard_map/reshape | solution.py:390
  0.8 0.7 %convert_element_type.7 = f32[2,256]{1,0:T(2,128)S(1)} convert(s32[2,256]{1,0:T(2,128)} %param.15) | non-fusion elementwise | flops 512 | bytes 4096 | tf_op jit(solution)/shard_map/convert_element_type | solution.py:385
  1.6 0.0 copy-done.5
  1.6 0.0 copy-start.2
  1.6 0.0 copy-start.3
  1.6 0.0 copy-start.4
  1.6 0.1 maximum_maximum_fusion.extra
  1.7 0.0 copy-done.1
  1.7 0.7 %copy-done.2 = bf16[256,128]{1,0:T(8,128)(2,1)S(1)} copy-done((bf16[256,128]{1,0:T(8,128)(2,1)S(1)}, bf16[256,128]{1,0:T(8,128)(2,1)}, u32[]{:S(2)}) %copy-start.2) | copy-done | bytes 65560
  2.4 0.0 copy-done.3
  2.4 0.0 copy-done.4
  2.4 0.0 copy-start
  2.4 1.2 %copy-done = bf16[2,2,7,128,128]{4,3,2,1,0:T(8,128)(2,1)S(1)} copy-done((bf16[2,2,7,128,128]{4,3,2,1,0:T(8,128)(2,1)S(1)}, bf16[2,2,7,128,128]{4,3,2,1,0:T(8,128)(2,1)}, u32[]{:S(2)}) %copy-start) | copy-done | bytes 917528
  3.6 52.6 %shard_map.82 = bf16[2,256,128]{2,1,0:T(8,128)(2,1)S(1)} custom-call(bf16[2,256,128]{2,1,0:T(8,128)(2,1)S(1)} %copy-done.1, bf16[2,2,7,128,128]{4,3,2,1,0:T(8,128)(2,1)S(1)} %copy-done, bf16[256,128]{1,0:T(8,128)(2,1)S(1)} %copy-done.2, f32[72,128]{1,0:T(8,128)S(1)} %maximum_maximum_fusion.extra, f32[1,128]{1,0:T(1,128)S(1)} %bitcast.9, ...), custom_call_target="tpu_custom_call" | custom-call | tf_op jit(solution)/shard_map/pallas_call | solution.py:393
  56.2 0.7 %copy.10 = bf16[2,256,128]{2,1,0:T(8,128)(2,1)} copy(bf16[2,256,128]{2,1,0:T(8,128)(2,1)S(1)} %shard_map.82) | data formatting | bytes 262144
  (4 shorter events, 0.0 us)
Async XLA Ops:
  0.0 1.6 %copy-start.5 = (f32[64,8,8]{0,2,1:T(8,128)S(1)}, f32[64,8,8]{0,2,1:T(8,128)}, u32[]{:S(2)}) copy-start(f32[64,8,8]{0,2,1:T(8,128)} %param.13) | copy-start | bytes 49156
  0.0 1.7 %copy-start.1 = (bf16[2,256,128]{2,1,0:T(8,128)(2,1)S(1)}, bf16[2,256,128]{2,1,0:T(8,128)(2,1)}, u32[]{:S(2)}) copy-start(bf16[2,256,128]{2,1,0:T(8,128)(2,1)} %tracer.1) | copy-start | bytes 393220
  1.6 0.8 %copy-start.2 = (bf16[256,128]{1,0:T(8,128)(2,1)S(1)}, bf16[256,128]{1,0:T(8,128)(2,1)}, u32[]{:S(2)}) copy-start(bf16[256,128]{1,0:T(8,128)(2,1)} %source.1) | copy-start | bytes 196612
  1.6 0.8 %copy-start.3 = (s32[2,2]{1,0:T(2,128)S(1)}, s32[2,2]{1,0:T(2,128)}, u32[]{:S(2)}) copy-start(s32[2,2]{1,0:T(2,128)} %counts.1) | copy-start | bytes 52
  1.6 0.8 %copy-start.4 = (f32[128]{0:T(128)S(1)}, f32[128]{0:T(128)}, u32[]{:S(2)}) copy-start(f32[128]{0:T(128)} %param.14) | copy-start | bytes 1540
  2.4 1.2 %copy-start = (bf16[2,2,7,128,128]{4,3,2,1,0:T(8,128)(2,1)S(1)}, bf16[2,2,7,128,128]{4,3,2,1,0:T(8,128)(2,1)}, u32[]{:S(2)}) copy-start(bf16[2,2,7,128,128]{4,3,2,1,0:T(8,128)(2,1)} %tiles.1) | copy-start | bytes 2752516

commit v2 on v1

--- a/solution.py
+++ b/solution.py
@@ -10,7 +10,19 @@
 REACH = 2
 STEPS = 4
 Q = 4
+ORDER = [
+    (late, p, q)
+    for when, late, p, q in sorted(
+        (6.8 * p + 3.0 * late + 1.05 * q, late, p, q)
+        for p in range(1, STEPS + 1)
+        for late in range(2)
+        for q in range(Q)
+        if p + late <= STEPS
+    )
+]
 MESH = pl.DeviceIdType.MESH
+ALL = ((1, 1, 1), (1, 1, 0), (1, 0, 0), (1, 0, 1), (0, 1, 1), (0, 1, 0), (0, 0, 1))
+SAME = ((1, 1, 1), (1, 0, 0), (0, 1, 1))
 F32 = jnp.float32
 BF16 = jnp.bfloat16
 
@@ -68,29 +80,34 @@
     core = lax.rem(v, 2)
     chip = v // 2
     base = 2 * chip
-    part = lax.rem(core + chip + h // 2 + lax.rem(h, 2), 2)
     partner = jnp.where(even, h + 1, h - 1)
     ahead = jnp.where(even, h + 2, h - 2)
     behind = jnp.where(even, h - 2, h + 2)
     has_ahead = (ahead >= 0) & (ahead < h_size)
     has_behind = (behind >= 0) & (behind < h_size)
+    part = lax.rem(core + chip + h // 2, 2)
+    central = lax.rem(core + chip, 2) == 1
+
+    def target(dy, dx, dc):
+        flipped = v
+        if dc:
+            flipped = flipped + 1 - 2 * core
+        if dx:
+            flipped = lax.rem(flipped + 2, 4)
+        return {"horiz": partner if dy else h, "vert": flipped}
 
     def vert(d):
-        flipped = v
-        if d & 1:
-            flipped = flipped + 1 - 2 * core
-        if d & 2:
-            flipped = lax.rem(flipped + 2, 4)
-        return {"horiz": h, "vert": flipped}
+        return target(0, d // 2, d % 2)
 
     crossed = v + 1 - 2 * core
-    near = {"horiz": partner, "vert": crossed}
     front = {"horiz": ahead, "vert": crossed}
     back = {"horiz": behind, "vert": crossed}
 
     barrier = pltpu.get_barrier_semaphore()
-    for where in (vert(1), vert(2), vert(3), near):
-        pl.semaphore_signal(barrier, inc=1, device_id=where, device_id_type=MESH)
+    for dy, dx, dc in ALL:
+        pl.semaphore_signal(
+            barrier, inc=1, device_id=target(dy, dx, dc), device_id_type=MESH
+        )
 
     @pl.when(has_ahead)
     def _():
@@ -118,30 +135,43 @@
             src, dst, send_sem.at[p, q, kind], recv_sem.at[p, q, kind], where
         )
 
-    def x_copies(p, q):
-        if p == 0:
-            here = gath.at[0, q, pl.ds(lev_dev * v, lev_dev)]
-            return [
-                copy_to(
-                    here if d == 3 else other.at[q],
-                    here,
-                    first_send.at[q, d - 1],
-                    first_recv.at[q, d - 1],
-                    vert(d),
-                )
-                for d in (3, 2, 1)
-            ]
-        here = gath.at[p % 2, q, pl.ds(lev_chip * chip, lev_chip)]
-        return [remote(here, here, p, q, 0, vert(3))]
+    def first_copy(q, n):
+        dy, dx, dc = ALL[n]
+        mine = gath.at[0, q, 0, pl.ds(lev_dev * v, lev_dev)]
+        return copy_to(
+            other.at[q] if (dx + dc) % 2 else mine,
+            gath.at[0, q, dy, pl.ds(lev_dev * v, lev_dev)],
+            first_send.at[q, n],
+            first_recv.at[q, n],
+            target(dy, dx, dc),
+        )
+
+    def first_all(q, sending, act):
+        for n, (dy, dx, dc) in enumerate(ALL):
+            if not dx:
+                act(first_copy(q, n))
+                continue
+            wanted = central if sending or dc else ~central
+
+            @pl.when(wanted)
+            def _():
+                act(first_copy(q, n))
+
+    def step_copy(p, q, n):
+        dy, dx, dc = SAME[n]
+        mine = gath.at[p % 2, q, 0, pl.ds(lev_chip * chip, lev_chip)]
+        theirs = gath.at[p % 2, q, dy, pl.ds(lev_chip * chip, lev_chip)]
+        return remote(mine, theirs, p, q, n, target(dy, dx, dc))
+
+    def step_copies(p, q):
+        kinds = (2,) if p == STEPS else (0, 1, 2)
+        return [step_copy(p, q, n) for n in kinds]
 
     def block(p, q, at):
         return halos[p % 2 * Q + q].at[pl.ds(at, blk)]
 
-    def near_copy(p, q):
-        return remote(block(p, q, blk), block(p, q, far_at), p, q, 1, near)
-
     def front_copy(p, q):
-        return remote(block(p, q, near_at), block(p, q, far_at), p, q, 2, front)
+        return remote(block(p, q, near_at), block(p, q, far_at), p, q, 3, front)
 
     def last_copies(q):
         theirs = lev_dev * (v + 1 - 2 * core) - base
@@ -170,7 +200,7 @@
             for t in range(tiles_dev):
                 ours = pl.ds(pl.multiple_of(part * half + q * ch, ch), ch)
                 theirs = pl.ds(pl.multiple_of((1 - part) * half + q * ch, ch), ch)
-                gath[0, q, lev_dev * v + level, t] = turned[level, t, ours, :]
+                gath[0, q, 0, lev_dev * v + level, t] = turned[level, t, ours, :]
                 other[q, level, t] = turned[level, t, theirs, :]
 
     def explicit(p, q):
@@ -189,41 +219,44 @@
                 if level == 0:
                     ours = pl.ds(pl.multiple_of(part * half + q * ch, ch), ch)
                     flow = flow + src_t[t, ours, :]
-                gath[p % 2, q, lev_chip * chip + level, t] = flow.astype(BF16)
+                gath[p % 2, q, 0, lev_chip * chip + level, t] = flow.astype(BF16)
 
     def stage_a(p, q):
         if p == 0:
             load_first(q)
+            first_all(q, True, lambda copy: copy.start())
+            return
+        if p == 1:
+            first_all(q, True, lambda copy: copy.wait_send())
         else:
-            explicit(p, q)
-        for copy in x_copies(p, q):
+            for copy in step_copies(p - 1, q):
+                copy.wait_send()
+
+        @pl.when(has_behind)
+        def _():
+            front_copy(p - 1, q).wait_recv()
+
+        explicit(p, q)
+        for copy in step_copies(p, q):
             copy.start()
 
-    def sends_done(p, q):
-        for copy in x_copies(p, q):
-            copy.wait_send()
-        if p == STEPS:
-            return
-        near_copy(p, q).wait_send()
-
-        @pl.when(has_ahead)
-        def _():
-            front_copy(p, q).wait_send()
-
-    def solve(p, q):
+    def solve(p, q, which):
         par = p % 2
         halo = halos[par * Q + q]
+        at0 = near_at if which else blk
         if p == 0:
             for t in range(tiles_dev):
                 for k in range(window):
-                    halo[blk + t * window + k] = gath[par, q, base + k, t]
+                    halo[at0 + t * window + k] = gath[par, q, which, base + k, t]
             return
         rows = 16
 
         for t in range(tiles_dev):
             for i in range(ch // rows):
                 at = slice(i * rows, (i + 1) * rows)
-                loaded = [gath[par, q, m, t, at, :].astype(F32) for m in range(levels)]
+                loaded = [
+                    gath[par, q, which, m, t, at, :].astype(F32) for m in range(levels)
+                ]
                 start = part * half + q * ch + i * rows
                 rate = fall[pl.ds(pl.multiple_of(start, rows), rows), :]
                 stay = 1.0 - rate
@@ -232,41 +265,46 @@
                     mixed = None
                     for m in range(levels):
                         r = k * levels + m
-                        term = a_win[t, r : r + 1, :] * loaded[m]
+                        term = a_win[which, t, r : r + 1, :] * loaded[m]
                         mixed = term if m == 0 else mixed + term
                     if k:
                         settled = stay * mixed + rate * above
-                        wet = w_win[t, k - 1 : k, :]
-                        halo[blk + t * window + k - 1, at, :] = (wet * settled).astype(BF16)
+                        wet = w_win[which, t, k - 1 : k, :]
+                        halo[at0 + t * window + k - 1, at, :] = (wet * settled).astype(
+                            BF16
+                        )
                     above = mixed
 
     def stage_b(p, q):
-        for copy in x_copies(p, q):
-            copy.wait_recv()
+        if p == 0:
+            first_all(q, False, lambda copy: copy.wait_recv())
+        elif p < STEPS:
+            step_copy(p, q, 0).wait_recv()
+            step_copy(p, q, 1).wait_recv()
         if p:
-            sends_done(p - 1, q)
-        solve(p, q)
+
+            @pl.when(has_ahead)
+            def _():
+                front_copy(p - 1, q).wait_send()
+
         if p < STEPS:
-            near_copy(p, q).start()
-        else:
+            solve(p, q, 1)
+
+            @pl.when(has_ahead)
+            def _():
+                front_copy(p, q).start()
+
+        if p:
+            step_copy(p, q, 2).wait_recv()
+        solve(p, q, 0)
+        if p == STEPS:
             for copy in last_copies(q):
                 copy.start()
 
-    def stage_c(p, q):
-        near_copy(p, q).wait_recv()
-
-        @pl.when(has_ahead)
-        def _():
-            front_copy(p, q).start()
-
-    def stage_d(p, q):
-        @pl.when(has_behind)
-        def _():
-            front_copy(p, q).wait_recv()
-
-    def ops_copy(d):
+    def ops_copy(n):
+        dy, dx, dc = ALL[n]
         return copy_to(
-            extra, ops.at[v], ops_send.at[d - 1], ops_recv.at[d - 1], vert(d)
+            extra, ops.at[dy, v], ops_send.at[n], ops_recv.at[n], target(dy, dx, dc)
         )
 
     def prepare():
@@ -298,56 +336,56 @@
 
     def operators():
         square = levels * levels
-        for t in range(tiles_dev):
-            for k in range(window + 1):
-                level = base + k - 1
-                row = pl.ds(
-                    pl.multiple_of(jnp.maximum(level, 0) * levels, levels), levels
-                )
-                keep = (level >= 0).astype(F32)
-                a_win[t, k * levels : (k + 1) * levels, :] = keep * (
-                    ops[2 * t, row, :] + ops[2 * t + 1, row, :]
-                )
-                if k:
-                    w_win[t, k - 1 : k, :] = ops[
-                        level // lev_dev,
-                        pl.ds(square + lax.rem(level, lev_dev) * tiles_dev + t, 1),
-                        :,
-                    ]
-
-    ops[v] = extra[...]
+        for which in range(2):
+            for t in range(tiles_dev):
+                for k in range(window + 1):
+                    level = base + k - 1
+                    row = pl.ds(
+                        pl.multiple_of(jnp.maximum(level, 0) * levels, levels), levels
+                    )
+                    keep = (level >= 0).astype(F32)
+                    a_win[which, t, k * levels : (k + 1) * levels, :] = keep * (
+                        ops[which, 2 * t, row, :] + ops[which, 2 * t + 1, row, :]
+                    )
+                    if k:
+                        w_win[which, t, k - 1 : k, :] = ops[
+                            which,
+                            level // lev_dev,
+                            pl.ds(square + lax.rem(level, lev_dev) * tiles_dev + t, 1),
+                            :,
+                        ]
+
+    ops[0, v] = extra[...]
     cols_v[core] = columns[...]
     for level in range(lev_dev):
         for t in range(tiles_dev):
             turned[level, t] = tracer[level, t * size : (t + 1) * size, :].T
-    count = 4 + has_ahead.astype(jnp.int32) + has_behind.astype(jnp.int32)
+    count = len(ALL) + has_ahead.astype(jnp.int32) + has_behind.astype(jnp.int32)
     pl.semaphore_wait(barrier, count)
     for q in range(Q):
         stage_a(0, q)
-    for d in (1, 2, 3):
-        ops_copy(d).start()
     pair = pair_copies()
     pair[0].start()
+    for n in range(len(ALL)):
+        ops_copy(n).start()
     prepare()
     pair[1].start()
     for q in range(Q):
         stage_b(0, q)
     prepare_more()
-    for d in (1, 2, 3):
-        ops_copy(d).wait()
-    operators()
     pair[0].wait()
     positions()
-    for p in range(STEPS):
-        for q in range(Q):
-            stage_c(p, q)
-        if p == 0:
-            pair[1].wait()
-        for q in range(Q):
-            stage_d(p, q)
+    pair[1].wait()
+    for q in range(Q):
+        stage_a(1, q)
+    for n in range(len(ALL)):
+        ops_copy(n).wait()
+    operators()
+    for late, p, q in ORDER:
+        if late:
             stage_a(p + 1, q)
-        for q in range(Q):
-            stage_b(p + 1, q)
+        else:
+            stage_b(p, q)
     mine = lev_dev * v - base
     for q in range(Q):
         for t in range(tiles_dev):
@@ -365,8 +403,7 @@
             )
             out[level, t * size : (t + 1) * size, :] = whole.T
     for q in range(Q):
-        sends_done(STEPS, q)
-        for copy in last_copies(q):
+        for copy in step_copies(STEPS, q) + last_copies(q):
             copy.wait_send()
 
 
@@ -398,25 +435,25 @@
         scratch_shapes=[
             pltpu.VMEM((2 * lev_dev, tiles_dev, slots * size, size), BF16),
             pltpu.VMEM((lev_dev, tiles_dev, classes, size), BF16),
-            pltpu.VMEM((2, Q, levels, tiles_dev, ch, size), BF16),
+            pltpu.VMEM((2, Q, 2, levels, tiles_dev, ch, size), BF16),
             pltpu.VMEM((Q, lev_dev, tiles_dev, ch, size), BF16),
             pltpu.VMEM((2 * Q, tiles_dev, lev_dev, ch, size), BF16),
             pltpu.VMEM((tiles_dev, classes, size), F32),
             pltpu.VMEM((classes, size), F32),
-            pltpu.VMEM((v_size,) + extra.shape, F32),
-            pltpu.VMEM((tiles_dev, (window + 1) * levels, size), F32),
-            pltpu.VMEM((tiles_dev, 8, size), F32),
+            pltpu.VMEM((2, v_size) + extra.shape, F32),
+            pltpu.VMEM((2, tiles_dev, (window + 1) * levels, size), F32),
+            pltpu.VMEM((2, tiles_dev, 8, size), F32),
             pltpu.VMEM((2,) + cols.shape, jnp.int32),
             pltpu.SMEM((2,) + cols.shape, jnp.int32),
             pltpu.SMEM((2 * lev_dev, tiles_dev * slots), jnp.int32),
-            dma((phases, Q, 3)),
-            dma((phases, Q, 3)),
-            dma((Q, 3)),
-            dma((Q, 3)),
+            dma((phases, Q, 4)),
+            dma((phases, Q, 4)),
+            dma((Q, len(ALL))),
+            dma((Q, len(ALL))),
             dma((Q, tiles_dev)),
             dma((Q, tiles_dev)),
-            dma((3,)),
-            dma((3,)),
+            dma((len(ALL),)),
+            dma((len(ALL),)),
             dma((2,)),
             dma((2,)),
             dma(()),

time: 57.1 us -> 49.6 us (0.87)
  Pallas kernels: 52.6 us -> 44.5 us
    pallas_call x1, Pallas kernels: 52.6 us -> 44.5 us  [on_device(): pl.pallas_call(functools.partial(kernel, h_size, v_size), out_shape=jax.S...]
where the time goes in v2:
time: 49.6 us; the launch traced here: 48.8 us
  Pallas kernels  44.5 us (90%)
  local copies, waits for them, and re-layouts  3.43 us (7%)
  other arithmetic  0.78 us (2%)
    pallas_call x1, Pallas kernels, on_device(): pl.pallas_call(functools.partial(kernel, h_size, v_size), out_shape=jax.S...  44.5 us
    unnamed x13, local copies, waits for them, and re-layouts  2.57 us

profile of v2, /device:TPU:0, one launch (start us, length us, event | category | flops | bytes accessed | tf_op | source)
XLA Modules:
  0.0 48.8 jit_solution(1079023913528624742)
XLA Ops:
  0.0 0.0 copy-start.5
  0.0 0.0 copy-start.1
  0.0 0.1 pad.8.clone
  0.1 0.8 %reshape.16 = s32[2,14]{1,0:T(2,128)S(1)} reshape(s32[2,2,7]{2,1,0:T(2,128)} %param.10) | data formatting | bytes 224 | tf_op jit(solution)/shard_map/reshape | solution.py:427
  0.8 0.7 %convert_element_type.7 = f32[2,256]{1,0:T(2,128)S(1)} convert(s32[2,256]{1,0:T(2,128)} %param.15) | non-fusion elementwise | flops 512 | bytes 4096 | tf_op jit(solution)/shard_map/convert_element_type | solution.py:422
  1.6 0.0 copy-done.5
  1.6 0.0 copy-start.2
  1.6 0.0 copy-start.3
  1.6 0.0 copy-start.4
  1.6 0.1 maximum_maximum_fusion.extra
  1.7 0.0 copy-done.1
  1.7 0.7 %copy-done.2 = bf16[256,128]{1,0:T(8,128)(2,1)S(1)} copy-done((bf16[256,128]{1,0:T(8,128)(2,1)S(1)}, bf16[256,128]{1,0:T(8,128)(2,1)}, u32[]{:S(2)}) %copy-start.2) | copy-done | bytes 65560
  2.4 0.0 copy-done.3
  2.4 0.0 copy-done.4
  2.4 0.0 copy-start
  2.4 1.2 %copy-done = bf16[2,2,7,128,128]{4,3,2,1,0:T(8,128)(2,1)S(1)} copy-done((bf16[2,2,7,128,128]{4,3,2,1,0:T(8,128)(2,1)S(1)}, bf16[2,2,7,128,128]{4,3,2,1,0:T(8,128)(2,1)}, u32[]{:S(2)}) %copy-start) | copy-done | bytes 917528
  3.6 44.5 %shard_map.82 = bf16[2,256,128]{2,1,0:T(8,128)(2,1)S(1)} custom-call(bf16[2,256,128]{2,1,0:T(8,128)(2,1)S(1)} %copy-done.1, bf16[2,2,7,128,128]{4,3,2,1,0:T(8,128)(2,1)S(1)} %copy-done, bf16[256,128]{1,0:T(8,128)(2,1)S(1)} %copy-done.2, f32[72,128]{1,0:T(8,128)S(1)} %maximum_maximum_fusion.extra, f32[1,128]{1,0:T(1,128)S(1)} %bitcast.9, ...), custom_call_target="tpu_custom_call" | custom-call | tf_op jit(solution)/shard_map/pallas_call | solution.py:430
  48.1 0.7 %copy.10 = bf16[2,256,128]{2,1,0:T(8,128)(2,1)} copy(bf16[2,256,128]{2,1,0:T(8,128)(2,1)S(1)} %shard_map.82) | data formatting | bytes 262144
  (4 shorter events, 0.0 us)
Async XLA Ops:
  0.0 1.6 %copy-start.5 = (f32[64,8,8]{0,2,1:T(8,128)S(1)}, f32[64,8,8]{0,2,1:T(8,128)}, u32[]{:S(2)}) copy-start(f32[64,8,8]{0,2,1:T(8,128)} %param.13) | copy-start | bytes 49156
  0.0 1.7 %copy-start.1 = (bf16[2,256,128]{2,1,0:T(8,128)(2,1)S(1)}, bf16[2,256,128]{2,1,0:T(8,128)(2,1)}, u32[]{:S(2)}) copy-start(bf16[2,256,128]{2,1,0:T(8,128)(2,1)} %tracer.1) | copy-start | bytes 393220
  1.6 0.8 %copy-start.2 = (bf16[256,128]{1,0:T(8,128)(2,1)S(1)}, bf16[256,128]{1,0:T(8,128)(2,1)}, u32[]{:S(2)}) copy-start(bf16[256,128]{1,0:T(8,128)(2,1)} %source.1) | copy-start | bytes 196612
  1.6 0.8 %copy-start.3 = (s32[2,2]{1,0:T(2,128)S(1)}, s32[2,2]{1,0:T(2,128)}, u32[]{:S(2)}) copy-start(s32[2,2]{1,0:T(2,128)} %counts.1) | copy-start | bytes 52
  1.6 0.8 %copy-start.4 = (f32[128]{0:T(128)S(1)}, f32[128]{0:T(128)}, u32[]{:S(2)}) copy-start(f32[128]{0:T(128)} %param.14) | copy-start | bytes 1540
  2.4 1.2 %copy-start = (bf16[2,2,7,128,128]{4,3,2,1,0:T(8,128)(2,1)S(1)}, bf16[2,2,7,128,128]{4,3,2,1,0:T(8,128)(2,1)}, u32[]{:S(2)}) copy-start(bf16[2,2,7,128,128]{4,3,2,1,0:T(8,128)(2,1)} %tiles.1) | copy-start | bytes 2752516

commit v3 on v2

--- a/solution.py
+++ b/solution.py
@@ -13,7 +13,7 @@
 ORDER = [
     (late, p, q)
     for when, late, p, q in sorted(
-        (6.8 * p + 3.0 * late + 1.05 * q, late, p, q)
+        (6.8 * p + 3.0 * late + 1.4 * q, late, p, q)
         for p in range(1, STEPS + 1)
         for late in range(2)
         for q in range(Q)
@@ -30,14 +30,23 @@
 def kernel(
     h_size,
     v_size,
+    tracer_hbm,
+    tiles_hbm,
+    columns_hbm,
+    counts_hbm,
+    source_hbm,
+    flat_hbm,
+    settling_hbm,
+    wet_hbm,
+    out,
     tracer,
     tiles,
+    counts,
     source,
+    flat,
+    settling,
+    wet,
     extra,
-    settling,
-    columns,
-    counts,
-    out,
     weights,
     turned,
     gath,
@@ -46,6 +55,7 @@
     src_t,
     fall,
     ops,
+    a_full,
     a_win,
     w_win,
     cols_v,
@@ -59,9 +69,12 @@
     last_recv,
     ops_send,
     ops_recv,
+    pass_send,
+    pass_recv,
     pair_send,
     pair_recv,
     local_sem,
+    load_sem,
     *halos,
 ):
     lev_dev, cells_dev, classes = tracer.shape
@@ -99,6 +112,24 @@
     def vert(d):
         return target(0, d // 2, d % 2)
 
+    loads = [
+        pltpu.make_async_copy(src, dst, load_sem.at[n])
+        for n, (src, dst) in enumerate(
+            (
+                (tracer_hbm, tracer),
+                (columns_hbm, cols_v.at[core]),
+                (flat_hbm, flat),
+                (wet_hbm, wet),
+                (counts_hbm, counts),
+                (settling_hbm, settling),
+                (source_hbm, source),
+                (tiles_hbm, tiles),
+            )
+        )
+    ]
+    for load in loads:
+        load.start()
+
     crossed = v + 1 - 2 * core
     front = {"horiz": ahead, "vert": crossed}
     back = {"horiz": behind, "vert": crossed}
@@ -223,7 +254,6 @@
 
     def stage_a(p, q):
         if p == 0:
-            load_first(q)
             first_all(q, True, lambda copy: copy.start())
             return
         if p == 1:
@@ -302,10 +332,36 @@
                 copy.start()
 
     def ops_copy(n):
-        dy, dx, dc = ALL[n]
+        dy, dx, dc = SAME[n]
         return copy_to(
             extra, ops.at[dy, v], ops_send.at[n], ops_recv.at[n], target(dy, dx, dc)
         )
+
+    def pass_copies():
+        across = v_size - 1 - v
+        return [
+            copy_to(
+                ops.at[dy, at],
+                ops.at[dy, at],
+                pass_send.at[dy, n],
+                pass_recv.at[dy, n],
+                vert(1),
+            )
+            for dy in range(2)
+            for n, at in enumerate((v, across))
+        ]
+
+    def pack():
+        rows = levels * levels // 2
+        extra[:rows, :] = jnp.concatenate([flat[:rows, :], flat[rows:, :]], axis=1)
+        extra[rows:, :] = jnp.zeros((8, size), F32)
+        for level in range(lev_dev):
+            for t in range(tiles_dev):
+                at = rows + level * tiles_dev + t
+                extra[at : at + 1, :] = wet[
+                    level : level + 1, t * size : (t + 1) * size
+                ].astype(F32)
+        ops[0, v] = extra[...]
 
     def prepare():
         for level in range(lev_dev):
@@ -329,57 +385,74 @@
         last = 3 * blk - 1
         for level in range(lev_chip):
             for n in range(tiles_dev * slots):
-                column = cols_s[level // lev_dev, level % lev_dev, n]
+                column = cols_s[
+                    level // lev_dev, level % lev_dev, n // slots, n % slots
+                ]
                 row = lax.div(column, h_tiles) - base
                 across = lax.rem(column, h_tiles) - tiles_dev * h + REACH
                 pos[level, n] = jnp.clip(across * window + row, 0, last)
 
     def operators():
-        square = levels * levels
+        rows = levels * levels // 2
         for which in range(2):
             for t in range(tiles_dev):
+                a = ops[which, 2 * t, :rows, :]
+                b = ops[which, 2 * t + 1, :rows, :]
+                on_left = lax.broadcasted_iota(jnp.int32, a.shape, 1) < size // 2
+                a_full[:levels, :] = jnp.zeros((levels, size), F32)
+                a_full[levels : levels + rows, :] = jnp.where(
+                    on_left, a, pltpu.roll(b, size // 2, 1)
+                )
+                a_full[levels + rows :, :] = jnp.where(
+                    on_left, pltpu.roll(a, size // 2, 1), b
+                )
                 for k in range(window + 1):
                     level = base + k - 1
-                    row = pl.ds(
-                        pl.multiple_of(jnp.maximum(level, 0) * levels, levels), levels
-                    )
-                    keep = (level >= 0).astype(F32)
-                    a_win[which, t, k * levels : (k + 1) * levels, :] = keep * (
-                        ops[which, 2 * t, row, :] + ops[which, 2 * t + 1, row, :]
-                    )
+                    row = pl.ds(pl.multiple_of((level + 1) * levels, levels), levels)
+                    a_win[which, t, k * levels : (k + 1) * levels, :] = a_full[row, :]
                     if k:
                         w_win[which, t, k - 1 : k, :] = ops[
                             which,
                             level // lev_dev,
-                            pl.ds(square + lax.rem(level, lev_dev) * tiles_dev + t, 1),
+                            pl.ds(rows + lax.rem(level, lev_dev) * tiles_dev + t, 1),
                             :,
                         ]
 
-    ops[0, v] = extra[...]
-    cols_v[core] = columns[...]
     for level in range(lev_dev):
         for t in range(tiles_dev):
+            if level == t == 0:
+                loads[0].wait()
             turned[level, t] = tracer[level, t * size : (t + 1) * size, :].T
+    for q in range(Q):
+        load_first(q)
     count = len(ALL) + has_ahead.astype(jnp.int32) + has_behind.astype(jnp.int32)
     pl.semaphore_wait(barrier, count)
     for q in range(Q):
         stage_a(0, q)
+    for load in loads[1:-1]:
+        load.wait()
     pair = pair_copies()
     pair[0].start()
-    for n in range(len(ALL)):
+    pack()
+    for n in range(len(SAME)):
         ops_copy(n).start()
+    loads[-1].wait()
     prepare()
     pair[1].start()
     for q in range(Q):
         stage_b(0, q)
+    for n in range(len(SAME)):
+        ops_copy(n).wait()
+    for copy in pass_copies():
+        copy.start()
     prepare_more()
     pair[0].wait()
     positions()
     pair[1].wait()
     for q in range(Q):
         stage_a(1, q)
-    for n in range(len(ALL)):
-        ops_copy(n).wait()
+    for copy in pass_copies():
+        copy.wait()
     operators()
     for late, p, q in ORDER:
         if late:
@@ -417,22 +490,26 @@
     assert lev_dev == 2 and tiles_dev == 2 and v_size == 4 and h_size % 2 == 0
     ch = classes // 2 // Q
     flat = implicit.reshape(share, levels * levels).T
-    right = lax.rem(lax.axis_index("vert"), 2).astype(F32)
-    flat = jnp.concatenate([flat * (1.0 - right), flat * right], axis=1)
-    wet_rows = wet.astype(F32).reshape(lev_dev * tiles_dev, size)
-    extra = jnp.concatenate([flat, wet_rows, jnp.zeros_like(wet_rows)], axis=0)
+    settling = settling.reshape(1, classes)
+    extra = (levels * levels // 2 + 8, size)
+    hbm = pl.BlockSpec(memory_space=pl.ANY)
     vm = pl.BlockSpec(memory_space=pltpu.VMEM)
-    sm = pl.BlockSpec(memory_space=pltpu.SMEM)
     phases = STEPS + 1
-    cols = columns.reshape(lev_dev, tiles_dev * slots)
-    cols = jnp.pad(cols, ((0, 8 - lev_dev), (0, 128 - cols.shape[1])))
     dma = pltpu.SemaphoreType.DMA
     return pl.pallas_call(
         functools.partial(kernel, h_size, v_size),
         out_shape=jax.ShapeDtypeStruct(tracer.shape, tracer.dtype),
-        in_specs=[vm] * 6 + [sm],
+        in_specs=[hbm] * 8,
         out_specs=vm,
         scratch_shapes=[
+            pltpu.VMEM(tracer.shape, BF16),
+            pltpu.VMEM(tiles.shape, BF16),
+            pltpu.SMEM(counts.shape, jnp.int32),
+            pltpu.VMEM(source.shape, BF16),
+            pltpu.VMEM(flat.shape, F32),
+            pltpu.VMEM(settling.shape, F32),
+            pltpu.VMEM(wet.shape, jnp.int32),
+            pltpu.VMEM(extra, F32),
             pltpu.VMEM((2 * lev_dev, tiles_dev, slots * size, size), BF16),
             pltpu.VMEM((lev_dev, tiles_dev, classes, size), BF16),
             pltpu.VMEM((2, Q, 2, levels, tiles_dev, ch, size), BF16),
@@ -440,11 +517,12 @@
             pltpu.VMEM((2 * Q, tiles_dev, lev_dev, ch, size), BF16),
             pltpu.VMEM((tiles_dev, classes, size), F32),
             pltpu.VMEM((classes, size), F32),
-            pltpu.VMEM((2, v_size) + extra.shape, F32),
+            pltpu.VMEM((2, v_size) + extra, F32),
+            pltpu.VMEM(((levels + 1) * levels, size), F32),
             pltpu.VMEM((2, tiles_dev, (window + 1) * levels, size), F32),
             pltpu.VMEM((2, tiles_dev, 8, size), F32),
-            pltpu.VMEM((2,) + cols.shape, jnp.int32),
-            pltpu.SMEM((2,) + cols.shape, jnp.int32),
+            pltpu.VMEM((2,) + columns.shape, jnp.int32),
+            pltpu.SMEM((2,) + columns.shape, jnp.int32),
             pltpu.SMEM((2 * lev_dev, tiles_dev * slots), jnp.int32),
             dma((phases, Q, 4)),
             dma((phases, Q, 4)),
@@ -452,17 +530,20 @@
             dma((Q, len(ALL))),
             dma((Q, tiles_dev)),
             dma((Q, tiles_dev)),
-            dma((len(ALL),)),
-            dma((len(ALL),)),
+            dma((len(SAME),)),
+            dma((len(SAME),)),
+            dma((2, 2)),
+            dma((2, 2)),
             dma((2,)),
             dma((2,)),
             dma(()),
+            dma((8,)),
         ]
         + [pltpu.VMEM((3 * tiles_dev * window, ch, size), BF16)] * (2 * Q),
         compiler_params=pltpu.CompilerParams(
-            collective_id=0, has_side_effects=True, vmem_limit_bytes=32 * 2**20
+            collective_id=0, has_side_effects=True, vmem_limit_bytes=56 * 2**20
         ),
-    )(tracer, tiles, source, extra, settling.reshape(1, classes), cols, counts)
+    )(tracer, tiles, columns, counts, source, flat, settling, wet)
 
 
 def solution(mesh):

time: 49.6 us -> 45.4 us (0.915); the launches traced: 48.8 us -> 45.1 us
  local copies, waits for them, and re-layouts: 3.43 us -> 1.57 us
  Pallas kernels: 44.5 us -> 43.5 us
  other arithmetic: 0.78 us -> 0 us
    pallas_call x1, Pallas kernels: 44.5 us -> 43.5 us  [on_device(): pl.pallas_call(functools.partial(kernel, h_size, v_size), out_shape=jax.S...]
    unnamed x13 -> x1, local copies, waits for them, and re-layouts: 2.57 us -> 1.57 us
    reshape x2 -> x0, local copies, waits for them, and re-layouts: 0.78 us -> none  [the longest x1 0.76 us: on_device(): cols = columns.reshape(lev_dev, tiles_dev * slots)]
    convert_element_type x1 -> x0, other arithmetic: 0.68 us -> none  [on_device(): wet_rows = wet.astype(F32).reshape(lev_dev * tiles_dev, size)]
where the time goes in v3:
time: 45.4 us; the launch traced here: 45.1 us
  Pallas kernels  43.5 us (96%)
  local copies, waits for them, and re-layouts  1.57 us (3%)
    pallas_call x1, Pallas kernels, on_device(): pl.pallas_call(functools.partial(kernel, h_size, v_size), out_shape=jax.S...  43.5 us
    unnamed x1, local copies, waits for them, and re-layouts  1.57 us

profile of v3, /device:TPU:0, one launch (start us, length us, event | category | flops | bytes accessed | tf_op | source)
XLA Modules:
  0.0 45.1 jit_solution(11586101584001395704)
XLA Ops:
  0.0 43.5 %shard_map.82 = bf16[2,256,128]{2,1,0:T(8,128)(2,1)} custom-call(bf16[2,256,128]{2,1,0:T(8,128)(2,1)} %tracer_hbm.1, bf16[2,2,7,128,128]{4,3,2,1,0:T(8,128)(2,1)} %tiles_hbm.1, s32[2,2,7]{2,1,0:T(2,128)} %columns_hbm.1, s32[2,2]{1,0:T(2,128)} %counts_hbm.1, bf16[256,128]{1,0:T(8,128)(2,1)} %source_hbm.1, f32[64,64]{1,0:T(8,128)} %bitcast.4, ...), custom_call_target="tpu_custom_call" | custom-call | tf_op jit(solution)/shard_map/pallas_call | solution.py:499
  43.5 1.6 %copy.10 = bf16[2,256,128]{2,1,0:T(8,128)(2,1)} copy(bf16[2,256,128]{2,1,0:T(8,128)(2,1)} %shard_map.82) | data formatting | bytes 262144

commit v4 on v3

--- a/solution.py
+++ b/solution.py
@@ -541,9 +541,16 @@
         ]
         + [pltpu.VMEM((3 * tiles_dev * window, ch, size), BF16)] * (2 * Q),
         compiler_params=pltpu.CompilerParams(
-            collective_id=0, has_side_effects=True, vmem_limit_bytes=56 * 2**20
+            collective_id=0, has_side_effects=True, vmem_limit_bytes=32 * 2**20
         ),
-    )(tracer, tiles, columns, counts, source, flat, settling, wet)
+    )(
+        *(
+            pltpu.with_memory_space_constraint(operand, pltpu.HBM)
+            for operand in (
+                tracer, tiles, columns, counts, source, flat, settling, wet
+            )
+        )
+    )
 
 
 def solution(mesh):

time: 45.4 us -> 44.4 us (0.978); the launches traced: 45.1 us -> 43.6 us
  local copies, waits for them, and re-layouts: 1.57 us -> 0.66 us
  Pallas kernels: 43.5 us -> 42.9 us
    unnamed x1, local copies, waits for them, and re-layouts: 1.57 us -> 0.66 us
    pallas_call x1, Pallas kernels: 43.5 us -> 42.9 us  [on_device(): pl.pallas_call(functools.partial(kernel, h_size, v_size), out_shape=jax.S...]
where the time goes in v4:
time: 44.4 us; the launch traced here: 43.6 us
  Pallas kernels  42.9 us (97%)
  local copies, waits for them, and re-layouts  0.66 us (1%)
    pallas_call x1, Pallas kernels, on_device(): pl.pallas_call(functools.partial(kernel, h_size, v_size), out_shape=jax.S...  42.9 us

profile of v4, /device:TPU:0, one launch (start us, length us, event | category | flops | bytes accessed | tf_op | source)
XLA Modules:
  0.0 43.6 jit_solution(11056071564603269720)
XLA Ops:
  0.0 42.9 %shard_map.82 = bf16[2,256,128]{2,1,0:T(8,128)(2,1)S(1)} custom-call(bf16[2,256,128]{2,1,0:T(8,128)(2,1)} %tracer_hbm.1, bf16[2,2,7,128,128]{4,3,2,1,0:T(8,128)(2,1)} %tiles_hbm.1, s32[2,2,7]{2,1,0:T(2,128)} %columns_hbm.1, s32[2,2]{1,0:T(2,128)} %counts_hbm.1, bf16[256,128]{1,0:T(8,128)(2,1)} %source_hbm.1, f32[64,64]{1,0:T(8,128)} %bitcast.4, ...), custom_call_target="tpu_custom_call" | custom-call | tf_op jit(solution)/shard_map/pallas_call | solution.py:499
  43.0 0.7 %copy.10 = bf16[2,256,128]{2,1,0:T(8,128)(2,1)} copy(bf16[2,256,128]{2,1,0:T(8,128)(2,1)S(1)} %shard_map.82) | data formatting | bytes 262144

commit v5 on v4

--- a/solution.py
+++ b/solution.py
@@ -112,6 +112,24 @@
     def vert(d):
         return target(0, d // 2, d % 2)
 
+    crossed = v + 1 - 2 * core
+    front = {"horiz": ahead, "vert": crossed}
+    back = {"horiz": behind, "vert": crossed}
+
+    barrier = pltpu.get_barrier_semaphore()
+    for dy, dx, dc in ALL:
+        pl.semaphore_signal(
+            barrier, inc=1, device_id=target(dy, dx, dc), device_id_type=MESH
+        )
+
+    @pl.when(has_ahead)
+    def _():
+        pl.semaphore_signal(barrier, inc=1, device_id=front, device_id_type=MESH)
+
+    @pl.when(has_behind)
+    def _():
+        pl.semaphore_signal(barrier, inc=1, device_id=back, device_id_type=MESH)
+
     loads = [
         pltpu.make_async_copy(src, dst, load_sem.at[n])
         for n, (src, dst) in enumerate(
@@ -129,24 +147,6 @@
     ]
     for load in loads:
         load.start()
-
-    crossed = v + 1 - 2 * core
-    front = {"horiz": ahead, "vert": crossed}
-    back = {"horiz": behind, "vert": crossed}
-
-    barrier = pltpu.get_barrier_semaphore()
-    for dy, dx, dc in ALL:
-        pl.semaphore_signal(
-            barrier, inc=1, device_id=target(dy, dx, dc), device_id_type=MESH
-        )
-
-    @pl.when(has_ahead)
-    def _():
-        pl.semaphore_signal(barrier, inc=1, device_id=front, device_id_type=MESH)
-
-    @pl.when(has_behind)
-    def _():
-        pl.semaphore_signal(barrier, inc=1, device_id=back, device_id_type=MESH)
 
     near_at = jnp.where(even, 2 * blk, 0)
     far_at = jnp.where(even, 0, 2 * blk)
@@ -439,17 +439,19 @@
     loads[-1].wait()
     prepare()
     pair[1].start()
-    for q in range(Q):
+    stage_b(0, 0)
+    prepare_more()
+    pair[0].wait()
+    positions()
+    for q in range(1, Q):
         stage_b(0, q)
+    pair[1].wait()
+    stage_a(1, 0)
     for n in range(len(SAME)):
         ops_copy(n).wait()
     for copy in pass_copies():
         copy.start()
-    prepare_more()
-    pair[0].wait()
-    positions()
-    pair[1].wait()
-    for q in range(Q):
+    for q in range(1, Q):
         stage_a(1, q)
     for copy in pass_copies():
         copy.wait()

time: 44.4 us -> 43.5 us (0.980)
  Pallas kernels: 42.9 us -> 42.3 us
    pallas_call x1, Pallas kernels: 42.9 us -> 42.3 us  [on_device(): pl.pallas_call(functools.partial(kernel, h_size, v_size), out_shape=jax.S...]
where the time goes in v5:
time: 43.5 us; the launch traced here: 43 us
  Pallas kernels  42.3 us (97%)
  local copies, waits for them, and re-layouts  0.66 us (2%)
    pallas_call x1, Pallas kernels, on_device(): pl.pallas_call(functools.partial(kernel, h_size, v_size), out_shape=jax.S...  42.3 us

profile of v5, /device:TPU:0, one launch (start us, length us, event | category | flops | bytes accessed | tf_op | source)
XLA Modules:
  0.0 43.0 jit_solution(18091372488795388300)
XLA Ops:
  0.0 42.3 %shard_map.82 = bf16[2,256,128]{2,1,0:T(8,128)(2,1)S(1)} custom-call(bf16[2,256,128]{2,1,0:T(8,128)(2,1)} %tracer_hbm.1, bf16[2,2,7,128,128]{4,3,2,1,0:T(8,128)(2,1)} %tiles_hbm.1, s32[2,2,7]{2,1,0:T(2,128)} %columns_hbm.1, s32[2,2]{1,0:T(2,128)} %counts_hbm.1, bf16[256,128]{1,0:T(8,128)(2,1)} %source_hbm.1, f32[64,64]{1,0:T(8,128)} %bitcast.4, ...), custom_call_target="tpu_custom_call" | custom-call | tf_op jit(solution)/shard_map/pallas_call | solution.py:501
  42.3 0.7 %copy.10 = bf16[2,256,128]{2,1,0:T(8,128)(2,1)} copy(bf16[2,256,128]{2,1,0:T(8,128)(2,1)S(1)} %shard_map.82) | data formatting | bytes 262144

commit v6 on v5

--- a/solution.py
+++ b/solution.py
@@ -256,6 +256,8 @@
         if p == 0:
             first_all(q, True, lambda copy: copy.start())
             return
+        if p > 1:
+            solve_own(p - 1, q)
         if p == 1:
             first_all(q, True, lambda copy: copy.wait_send())
         else:
@@ -305,6 +307,11 @@
                         )
                     above = mixed
 
+    def solve_own(p, q):
+        if p:
+            step_copy(p, q, 2).wait_recv()
+        solve(p, q, 0)
+
     def stage_b(p, q):
         if p == 0:
             first_all(q, False, lambda copy: copy.wait_recv())
@@ -324,9 +331,8 @@
             def _():
                 front_copy(p, q).start()
 
-        if p:
-            step_copy(p, q, 2).wait_recv()
-        solve(p, q, 0)
+        if p == 0 or p == STEPS:
+            solve_own(p, q)
         if p == STEPS:
             for copy in last_copies(q):
                 copy.start()
@@ -425,22 +431,23 @@
             turned[level, t] = tracer[level, t * size : (t + 1) * size, :].T
     for q in range(Q):
         load_first(q)
+    for load in loads[1:-1]:
+        load.wait()
+    pack()
+    prepare_more()
     count = len(ALL) + has_ahead.astype(jnp.int32) + has_behind.astype(jnp.int32)
     pl.semaphore_wait(barrier, count)
-    for q in range(Q):
+    stage_a(0, 0)
+    for q in range(1, Q):
         stage_a(0, q)
-    for load in loads[1:-1]:
-        load.wait()
+    for n in range(len(SAME)):
+        ops_copy(n).start()
     pair = pair_copies()
     pair[0].start()
-    pack()
-    for n in range(len(SAME)):
-        ops_copy(n).start()
     loads[-1].wait()
     prepare()
     pair[1].start()
     stage_b(0, 0)
-    prepare_more()
     pair[0].wait()
     positions()
     for q in range(1, Q):
@@ -451,11 +458,12 @@
         ops_copy(n).wait()
     for copy in pass_copies():
         copy.start()
-    for q in range(1, Q):
-        stage_a(1, q)
+    stage_a(1, 1)
+    stage_a(1, 2)
     for copy in pass_copies():
         copy.wait()
     operators()
+    stage_a(1, 3)
     for late, p, q in ORDER:
         if late:
             stage_a(p + 1, q)

time: 43.5 us -> 43.1 us (level)
  no operation moved by 1% of the time
where the time goes in v6:
time: 43.1 us; the launch traced here: 42.9 us
  Pallas kernels  42.2 us (98%)
  local copies, waits for them, and re-layouts  0.66 us (2%)
    pallas_call x1, Pallas kernels, on_device(): pl.pallas_call(functools.partial(kernel, h_size, v_size), out_shape=jax.S...  42.2 us

profile of v6, /device:TPU:0, one launch (start us, length us, event | category | flops | bytes accessed | tf_op | source)
XLA Modules:
  0.0 42.9 jit_solution(11948756728239123660)
XLA Ops:
  0.0 42.2 %shard_map.82 = bf16[2,256,128]{2,1,0:T(8,128)(2,1)S(1)} custom-call(bf16[2,256,128]{2,1,0:T(8,128)(2,1)} %tracer_hbm.1, bf16[2,2,7,128,128]{4,3,2,1,0:T(8,128)(2,1)} %tiles_hbm.1, s32[2,2,7]{2,1,0:T(2,128)} %columns_hbm.1, s32[2,2]{1,0:T(2,128)} %counts_hbm.1, bf16[256,128]{1,0:T(8,128)(2,1)} %source_hbm.1, f32[64,64]{1,0:T(8,128)} %bitcast.4, ...), custom_call_target="tpu_custom_call" | custom-call | tf_op jit(solution)/shard_map/pallas_call | solution.py:509
  42.2 0.7 %copy.10 = bf16[2,256,128]{2,1,0:T(8,128)(2,1)} copy(bf16[2,256,128]{2,1,0:T(8,128)(2,1)S(1)} %shard_map.82) | data formatting | bytes 262144

commit v7 on v6

--- a/solution.py
+++ b/solution.py
@@ -21,7 +21,7 @@
     )
 ]
 MESH = pl.DeviceIdType.MESH
-ALL = ((1, 1, 1), (1, 1, 0), (1, 0, 0), (1, 0, 1), (0, 1, 1), (0, 1, 0), (0, 0, 1))
+ALL = ((1, 1, 0), (1, 1, 1), (1, 0, 0), (1, 0, 1), (0, 1, 0), (0, 1, 1), (0, 0, 1))
 SAME = ((1, 1, 1), (1, 0, 0), (0, 1, 1))
 F32 = jnp.float32
 BF16 = jnp.bfloat16
@@ -195,7 +195,7 @@
         return remote(mine, theirs, p, q, n, target(dy, dx, dc))
 
     def step_copies(p, q):
-        kinds = (2,) if p == STEPS else (0, 1, 2)
+        kinds = (2,) if p == STEPS else (0, 2, 1)
         return [step_copy(p, q, n) for n in kinds]
 
     def block(p, q, at):

time: 43.1 us -> 43.1 us (level)
  no operation moved by 1% of the time
where the time goes in v7:
time: 43.1 us; the launch traced here: 43 us
  Pallas kernels  42.3 us (98%)
  local copies, waits for them, and re-layouts  0.66 us (2%)
    pallas_call x1, Pallas kernels, on_device(): pl.pallas_call(functools.partial(kernel, h_size, v_size), out_shape=jax.S...  42.3 us

profile of v7, /device:TPU:0, one launch (start us, length us, event | category | flops | bytes accessed | tf_op | source)
XLA Modules:
  0.0 43.0 jit_solution(11682919404976331950)
XLA Ops:
  0.0 42.3 %shard_map.82 = bf16[2,256,128]{2,1,0:T(8,128)(2,1)S(1)} custom-call(bf16[2,256,128]{2,1,0:T(8,128)(2,1)} %tracer_hbm.1, bf16[2,2,7,128,128]{4,3,2,1,0:T(8,128)(2,1)} %tiles_hbm.1, s32[2,2,7]{2,1,0:T(2,128)} %columns_hbm.1, s32[2,2]{1,0:T(2,128)} %counts_hbm.1, bf16[256,128]{1,0:T(8,128)(2,1)} %source_hbm.1, f32[64,64]{1,0:T(8,128)} %bitcast.4, ...), custom_call_target="tpu_custom_call" | custom-call | tf_op jit(solution)/shard_map/pallas_call | solution.py:509
  42.3 0.7 %copy.10 = bf16[2,256,128]{2,1,0:T(8,128)(2,1)} copy(bf16[2,256,128]{2,1,0:T(8,128)(2,1)S(1)} %shard_map.82) | data formatting | bytes 262144

commit v8 on v7

--- a/solution.py
+++ b/solution.py
@@ -435,6 +435,8 @@
         load.wait()
     pack()
     prepare_more()
+    loads[-1].wait()
+    prepare()
     count = len(ALL) + has_ahead.astype(jnp.int32) + has_behind.astype(jnp.int32)
     pl.semaphore_wait(barrier, count)
     stage_a(0, 0)
@@ -444,8 +446,6 @@
         ops_copy(n).start()
     pair = pair_copies()
     pair[0].start()
-    loads[-1].wait()
-    prepare()
     pair[1].start()
     stage_b(0, 0)
     pair[0].wait()

time: 43.1 us -> 43 us (level)
  no operation moved by 1% of the time
where the time goes in v8:
time: 43 us; the launch traced here: 42.9 us
  Pallas kernels  42.2 us (98%)
  local copies, waits for them, and re-layouts  0.66 us (2%)
    pallas_call x1, Pallas kernels, on_device(): pl.pallas_call(functools.partial(kernel, h_size, v_size), out_shape=jax.S...  42.2 us

profile of v8, /device:TPU:0, one launch (start us, length us, event | category | flops | bytes accessed | tf_op | source)
XLA Modules:
  0.0 42.9 jit_solution(3165395442154542280)
XLA Ops:
  0.0 42.2 %shard_map.82 = bf16[2,256,128]{2,1,0:T(8,128)(2,1)S(1)} custom-call(bf16[2,256,128]{2,1,0:T(8,128)(2,1)} %tracer_hbm.1, bf16[2,2,7,128,128]{4,3,2,1,0:T(8,128)(2,1)} %tiles_hbm.1, s32[2,2,7]{2,1,0:T(2,128)} %columns_hbm.1, s32[2,2]{1,0:T(2,128)} %counts_hbm.1, bf16[256,128]{1,0:T(8,128)(2,1)} %source_hbm.1, f32[64,64]{1,0:T(8,128)} %bitcast.4, ...), custom_call_target="tpu_custom_call" | custom-call | tf_op jit(solution)/shard_map/pallas_call | solution.py:509
  42.2 0.7 %copy.10 = bf16[2,256,128]{2,1,0:T(8,128)(2,1)} copy(bf16[2,256,128]{2,1,0:T(8,128)(2,1)S(1)} %shard_map.82) | data formatting | bytes 262144
